TPU v7x, 512 devices: a whole 4x8x8 slice. The times are simulated.
512 devices in a mesh: outer: 64 (over x, y_hi, z), node: 8 (over y_lo, core).
Axes of the slice: x: 4, y: 8 (y_hi: 2, y_lo: 4; y = y_hi * 4 + y_lo), z: 8, core: 2. Of those that a mesh axis runs over, the one named last changes fastest.
Arguments:
- hidden: bfloat16 [131072, 4096], P(('outer', 'node')), may hold values from -24 to 24
- codes: bfloat16 [4096, 256], P(('node', 'outer')), may hold values from -4 to 4
- scales: float32 [2, 256], replicated, may hold values from 0.008 to 0.032
- cotangent: bfloat16 [131072, 256], P(('outer', 'node')), may hold values from -6 to 6
Outputs:
- projected: bfloat16 [131072, 256], P(('outer', 'node'))
- grad_hidden: bfloat16 [131072, 4096], P(('outer', 'node'))
- grad_weight: float32 [4096, 256], P(('node', 'outer'))
All inputs are finite; a program needn't handle non-finite values.
Results may differ from a plain program's by a relative error of at most 0.017.
Values may be sent and summed in bfloat16 or wider, within the bound.
No kernel may reach another device: no remote copies, remote signals or barrier semaphores. Data moves between devices by JAX's collectives and lax.ppermute only.
A program may use at most 64 MiB of HBM per device.

v0:
```python
import jax
import jax.numpy as jnp
from jax import lax
from jax.sharding import PartitionSpec as P

BLOCK = 2048


def dequantize(piece, scales, start):
    count = piece.shape[0]
    row_ids = start + jnp.arange(count, dtype=jnp.int32)
    block_ids = row_ids // BLOCK
    onehot = (block_ids[:, None] == jnp.arange(scales.shape[0], dtype=jnp.int32)[None, :]).astype(
        jnp.float32
    )
    row_scales = jnp.dot(
        onehot, scales, precision=lax.Precision.HIGHEST, preferred_element_type=jnp.float32
    )
    return (piece.astype(jnp.float32) * row_scales).astype(jnp.bfloat16)


def body(hidden, codes, scales, cotangent):
    width = hidden.shape[1]
    n_node = lax.axis_size("node")
    node_idx = lax.axis_index("node")
    share = width // n_node
    secondary_codes = lax.all_gather(codes, "outer", axis=0, tiled=True)
    secondary = dequantize(secondary_codes, scales, node_idx * share)
    whole = lax.all_gather(secondary, "node", axis=0, tiled=True)
    projected = jnp.dot(hidden, whole, preferred_element_type=jnp.float32).astype(jnp.bfloat16)
    grad_hidden = lax.dot_general(
        cotangent,
        lax.all_gather(secondary, "node", axis=0, tiled=True),
        (((1,), (1,)), ((), ())),
        preferred_element_type=jnp.float32,
    ).astype(jnp.bfloat16)
    node_sums = lax.psum_scatter(
        lax.dot_general(
            hidden, cotangent, (((0,), (0,)), ((), ())), preferred_element_type=jnp.float32
        ).astype(jnp.bfloat16),
        "node",
        scatter_dimension=0,
        tiled=True,
    )
    grad_weight = lax.psum_scatter(
        node_sums.astype(jnp.float32), "outer", scatter_dimension=0, tiled=True
    )
    return (projected, grad_hidden, grad_weight)


def solution(mesh):
    placed = (
        P(("outer", "node"), None),
        P(("node", "outer"), None),
        P(),
        P(("outer", "node"), None),
    )
    return jax.shard_map(
        body,
        mesh=mesh,
        in_specs=placed,
        out_specs=(
            P(("outer", "node"), None),
            P(("outer", "node"), None),
            P(("node", "outer"), None),
        ),
        check_vma=False,
    )
```

profile of v0, /device:TPU:8, one launch (start us, length us, event | category | flops | bytes accessed | tf_op | source)
XLA Modules:
  0.0 728.1 jit_solution(12190243928124751157)
XLA Ops:
  7.2 0.0 copy-start
  7.2 0.0 reduce-scatter.3.cloned.1.call-start
  7.2 1.5 copy-done
  8.8 3.0 convolution_convert_fusion
  11.7 0.0 copy-start.2
  11.7 0.0 copy-start.3
  11.7 0.0 reduce-scatter.3.cloned.1.call-update
  11.8 0.0 all-gather.2.cloned.1.call-start
  11.8 0.6 copy-done.2
  12.4 230.0 %all_gather.7 = bf16[512,256]{1,0:T(8,128)(2,1)S(1)} all-gather(bf16[8,256]{1,0:T(8,128)(2,1)S(1)} %copy-done.2), channel_id=1, replica_groups=mesh['outer'=64,'node'=8] {'outer'}, dimensions={0}, use_global_device_ids=true | all-gather | bytes 266240 | tf_op jit(solution)/shard_map/all_gather | solution.py:27
  242.4 0.0 copy-done.3
  242.4 1.1 fusion.1
  243.5 0.0 all-gather.2.cloned.1.call-update
  243.5 0.0 reduce-scatter.5.cloned.1.call-start
  243.6 0.0 reduce-scatter.3.cloned.1.call-done
  243.6 1.8 convert_element_type.32
  245.4 0.0 reduce-scatter.5.cloned.1.call-update
  245.4 27.0 %all-gather.2.cloned.1.call-done = bf16[4096,256]{1,0:T(8,128)(2,1)} async-done(((bf16[512,256]{1,0:T(8,128)(2,1)}), bf16[4096,256]{1,0:T(8,128)(2,1)}) %all-gather.2.cloned.1.call-update) | async-done | bytes 2097168 | tf_op jit(solution)/shard_map/all_gather | solution.py:29
  272.4 0.0 copy-done.1
  272.4 3.6 fusion
  276.1 4.1 copy.8
  280.1 2.3 fusion.2
  282.5 0.8 copy.7
  283.2 438.3 %reduce-scatter.5.cloned.1.call-done = f32[8,256]{1,0:T(8,128)} async-done(((f32[512,256]{1,0:T(8,128)}), f32[8,256]{1,0:T(8,128)}) %reduce-scatter.5.cloned.1.call-update) | async-done | bytes 8208 | tf_op jit(solution)/shard_map/reduce_scatter | solution.py:45
  (2 shorter events, 0.0 us)
Async XLA Ops:
  7.2 1.6 copy-start
  7.2 236.4 %reduce-scatter.3.cloned.1.call-start = ((), (), s32[]{:S(2)}) async-start(), calls=%async_computation.3 | async-start | bytes 2359296 | tf_op jit(solution)/shard_map/reduce_scatter | solution.py:37
  11.7 0.7 copy-start.2
  11.7 230.6 %copy-start.3 = (f32[2,256]{1,0:T(2,128)S(1)}, f32[2,256]{1,0:T(2,128)}, u32[]{:S(2)}) copy-start(f32[2,256]{1,0:T(2,128)} %param.6) | copy-start | bytes 6148
  11.7 260.7 %copy-start.1 = (bf16[256,256]{1,0:T(8,128)(2,1)S(1)}, bf16[256,256]{1,0:T(8,128)(2,1)}, u32[]{:S(2)}) copy-start(bf16[256,256]{1,0:T(8,128)(2,1)} %param.7) | copy-start | bytes 393220
  11.8 260.6 %all-gather.2.cloned.1.call-start = ((), (), s32[]{:S(2)}) async-start(), calls=%async_computation.2 | async-start | bytes 2359296 | tf_op jit(solution)/shard_map/all_gather | solution.py:29
  243.5 478.0 %reduce-scatter.5.cloned.1.call-start = ((), (), s32[]{:S(2)}) async-start(), calls=%async_computation.4 | async-start | bytes 532480 | tf_op jit(solution)/shard_map/reduce_scatter | solution.py:45
Sparse Core Ops, SparseCore 0:
  11.9 44.6 reduce-scatter.2
  243.7 28.7 all-gather.1
  275.8 445.7 reduce-scatter.4
where the time goes:
time: 728 us
  waiting for transfers between devices  465 us (64%)
  blocking collectives  230 us (32%)
  between operations  13.8 us (2%)
  matrix products  10.1 us (1%)
    reduce_scatter x1, waiting for transfers between devices, body(): lax.psum_scatter(node_sums.astype(jnp.float32), 'outer', scatter_dimensio...  438 us
    all_gather x1, blocking collectives, body(): secondary_codes = lax.all_gather(codes, 'outer', axis=0, tiled=True)  230 us
    all_gather x1, waiting for transfers between devices, body(): whole = lax.all_gather(secondary, 'node', axis=0, tiled=True)  27 us
  transfers between devices with their start and end apart: 3, of which 2 were waited for; matrix products, arithmetic and copies ran while one was open for 2% of the time, Pallas kernels for 0%

commit v1 on v0

v1 whole, which is shorter than its diff:
```python
import jax
import jax.numpy as jnp
from jax import lax
from jax.sharding import Mesh, PartitionSpec as P

BLOCK = 2048
TORUS = ("yl", "yh", "z")


def exchange(pieces, axis):
    return lax.all_to_all(pieces, axis, 0, 0, tiled=True)


def swap(value):
    return lax.ppermute(value, "c", [(0, 1), (1, 0)])


def body(hidden, codes, scales, cotangent):
    tokens, width = hidden.shape
    rows, cols = codes.shape
    core = lax.axis_index("c")
    f32, bf16 = jnp.float32, jnp.bfloat16

    start = (lax.axis_index("yl") * 2 + core) * (width // 8)
    scale = lax.dynamic_index_in_dim(scales, start // BLOCK, 0, keepdims=True)
    own = (codes.astype(f32) * scale).astype(bf16)
    plane = exchange(jnp.broadcast_to(own[None], (64, rows, cols)), TORUS)
    plane = plane.reshape(1, 64 * rows, cols)
    half = exchange(jnp.broadcast_to(plane, (4,) + plane.shape[1:]), "x")
    half = half.reshape(4, 4, 16 * rows, cols).transpose(1, 0, 2, 3).reshape(4, width // 8, cols)
    other = swap(half)

    parts = hidden.reshape(tokens, 4, 2, width // 8)
    keep = lax.dynamic_index_in_dim(parts, core, 2, keepdims=False).reshape(tokens, width // 2)
    give = lax.dynamic_index_in_dim(parts, 1 - core, 2, keepdims=False).reshape(tokens, width // 2)
    got = swap(give)
    cot_other = swap(cotangent)
    both = jnp.concatenate([keep, got], axis=0)
    cots = jnp.concatenate([cotangent, cot_other], axis=0)
    term = lax.dot_general(both, cots, (((0,), (0,)), ((), ())), preferred_element_type=f32).astype(bf16)
    term = term.reshape(4, 4, 16 * rows, cols).transpose(1, 0, 2, 3).reshape(4, 64 * rows, cols)
    sums = jnp.sum(exchange(term, "x").astype(f32), axis=0).astype(bf16)
    grad_weight = jnp.sum(exchange(sums.reshape(64, rows, cols), TORUS).astype(f32), axis=0)

    first = jnp.where(core == 0, half, other)
    second = jnp.where(core == 0, other, half)
    whole = jnp.stack([first, second], axis=1).reshape(width, cols)
    projected = jnp.dot(hidden, whole, preferred_element_type=f32).astype(bf16)
    grad_hidden = lax.dot_general(
        cotangent, whole, (((1,), (1,)), ((), ())), preferred_element_type=f32
    ).astype(bf16)
    return projected, grad_hidden, grad_weight


def solution(mesh):
    fine = Mesh(mesh.devices.reshape(4, 2, 8, 4, 2), ("x", "yh", "z", "yl", "c"))
    outer, node = ("x", "yh", "z"), ("yl", "c")
    tokens, rows = P(outer + node, None), P(node + outer, None)
    return jax.shard_map(
        body,
        mesh=fine,
        in_specs=(tokens, rows, P(), tokens),
        out_specs=(tokens, tokens, rows),
        check_vma=False,
    )
```

time: 728 us -> 101 us (0.14)
  waiting for transfers between devices: 465 us -> 38.4 us
  blocking collectives: 230 us -> 0 us
  starting transfers between devices: 0.12 us -> 37.5 us
  between operations: 13.8 us -> 0.79 us
    reduce_scatter x2 -> x0, waiting for transfers between devices: 438 us -> none  [the longest x1 438 us: body(): lax.psum_scatter(node_sums.astype(jnp.float32), 'outer', scatter_dimensio...]
    all_gather x1 -> x0, blocking collectives: 230 us -> none  [body(): secondary_codes = lax.all_gather(codes, 'outer', axis=0, tiled=True)]
    all_to_all x0 -> x4, waiting for transfers between devices: none -> 38.3 us  [exchange(): return lax.all_to_all(pieces, axis, 0, 0, tiled=True)]
    all_to_all x0 -> x4, starting transfers between devices: none -> 31.6 us  [exchange(): return lax.all_to_all(pieces, axis, 0, 0, tiled=True)]
    all_gather x1 -> x0, waiting for transfers between devices: 27 us -> none  [body(): whole = lax.all_gather(secondary, 'node', axis=0, tiled=True)]
  transfers between devices with their start and end apart: 3 -> 7, of which waited for: 2 -> 4; matrix products, arithmetic and copies ran while one was open for 2% -> 20% of each run, Pallas kernels for 0% -> 0%
where the time goes in v1:
time: 101 us; the launch traced here: 99.8 us
  waiting for transfers between devices  38.4 us (38%)
  starting transfers between devices  37.5 us (37%)
  local copies, waits for them, and re-layouts  13 us (13%)
  matrix products  6.37 us (6%)
  other arithmetic  3.82 us (4%)
    all_to_all x4, waiting for transfers between devices, exchange(): return lax.all_to_all(pieces, axis, 0, 0, tiled=True)  38.3 us
    all_to_all x4, starting transfers between devices, exchange(): return lax.all_to_all(pieces, axis, 0, 0, tiled=True)  31.6 us
    unnamed x7, local copies, waits for them, and re-layouts  8.76 us
    ppermute x3, starting transfers between devices, swap(): return lax.ppermute(value, 'c', [(0, 1), (1, 0)])  5.87 us
    dot_general x1, matrix products, body(): projected = jnp.dot(hidden, whole, preferred_element_type=f32).astype(bf16)  2.37 us
    dot_general x1, matrix products, body(): lax.dot_general(cotangent, whole, (((1,), (1,)), ((), ())), preferred_ele...  2.08 us
  transfers between devices with their start and end apart: 7, of which 4 were waited for; matrix products, arithmetic and copies ran while one was open for 20% of the time, Pallas kernels for 0%

profile of v1, /device:TPU:8, one launch (start us, length us, event | category | flops | bytes accessed | tf_op | source)
XLA Modules:
  0.0 99.8 jit_solution(5339441252443445857)
XLA Ops:
  1.3 0.7 multiply_convert_fusion
  2.0 0.7 broadcast_in_dim.6
  2.7 16.6 %all-to-all-start = ((bf16[64,8,256]{2,1,0:T(8,128)(2,1)}), bf16[64,8,256]{2,1,0:T(8,128)(2,1)S(1)}, u32[]{:S(2)}, u32[]{:S(2)}) async-start(bf16[64,8,256]{2,1,0:T(8,128)(2,1)} %broadcast_in_dim.6), calls=%async_computation | async-start | bytes 524288 | tf_op jit(solution)/shard_map/all_to_all | solution.py:11
  19.3 3.3 %copy.21 = bf16[256,4096]{0,1:T(8,128)(2,1)S(1)} copy(bf16[256,4096]{1,0:T(8,128)(2,1)} %param.4) | data formatting | bytes 4194304 | tf_op args[0]
  22.6 1.2 %constant_dynamic-slice_fusion.1 = (bf16[256,4,1,512]{0,3,2,1:T(8,128)(2,1)S(1)}, bf16[256,4,1,512]{0,3,2,1:T(8,128)(2,1)}) fusion(bf16[256,4,2,512]{0,3,2,1:T(8,128)(2,1)S(1)} %bitcast.31, s32[]{:T(128)S(6)} %select_n.33, s32[]{:T(128)S(6)} %select_n.34), kind=kLoop, calls=%fused_computation.17 | loop fusion | bytes 4194312 | tf_op jit(solution)/shard_map/jit(dynamic_index_in_dim)/dynamic_slice | solution.py:34
  23.8 2.0 %collective-permute-start.1 = (bf16[256,2048]{0,1:T(8,128)(2,1)}, bf16[256,2048]{0,1:T(8,128)(2,1)}, u32[]{:S(2)}, u32[]{:S(2)}) collective-permute-start(bf16[256,2048]{0,1:T(8,128)(2,1)} %bitcast.12), channel_id=1, source_target_pairs={{0,1},{1,0},{2,3},{3,2},{4,5},{5,4},{6,7},{7,6},{8,9},{9,8},{10,11... | collective-permute-start | bytes 3145736 | tf_op jit(solution)/shard_map/ppermute | solution.py:15
  25.8 7.8 %all-to-all-done = bf16[64,8,256]{2,1,0:T(8,128)(2,1)S(1)} async-done(((bf16[64,8,256]{2,1,0:T(8,128)(2,1)}), bf16[64,8,256]{2,1,0:T(8,128)(2,1)S(1)}, u32[]{:S(2)}, u32[]{:S(2)}) %all-to-all-start) | async-done | bytes 262176 | tf_op jit(solution)/shard_map/all_to_all | solution.py:11
  33.6 1.0 %broadcast_in_dim.15 = bf16[4,512,256]{2,1,0:T(8,128)(2,1)} broadcast(bf16[512,256]{1,0:T(8,128)(2,1)S(1)} %bitcast.35), dimensions={1,2} | broadcast | bytes 1310720 | tf_op jit(solution)/shard_map/broadcast_in_dim | solution.py:29
  34.6 4.3 %all-to-all-start.1 = ((bf16[4,512,256]{2,1,0:T(8,128)(2,1)}), bf16[4,512,256]{2,1,0:T(8,128)(2,1)S(1)}, u32[]{:S(2)}, u32[]{:S(2)}) async-start(bf16[4,512,256]{2,1,0:T(8,128)(2,1)} %broadcast_in_dim.15), calls=%async_computation.1 | async-start | bytes 2097152 | tf_op jit(solution)/shard_map/all_to_all | solution.py:11
  38.9 1.9 %collective-permute-start.2 = (bf16[256,256]{1,0:T(8,128)(2,1)S(1)}, bf16[256,256]{1,0:T(8,128)(2,1)S(1)}, u32[]{:S(2)}, u32[]{:S(2)}) collective-permute-start(bf16[256,256]{1,0:T(8,128)(2,1)S(1)} %copy-done.1), channel_id=1, source_target_pairs={{0,1},{1,0},{2,3},{3,2},{4,5},{5,4},{6,7},{7,6},{8,9},{9,8},{10,11... | collective-permute-start | bytes 393224 | tf_op jit(solution)/shard_map/ppermute | solution.py:15
  40.9 11.5 %all-to-all-done.1 = bf16[4,512,256]{2,1,0:T(8,128)(2,1)S(1)} async-done(((bf16[4,512,256]{2,1,0:T(8,128)(2,1)}), bf16[4,512,256]{2,1,0:T(8,128)(2,1)S(1)}, u32[]{:S(2)}, u32[]{:S(2)}) %all-to-all-start.1) | async-done | bytes 1048608 | tf_op jit(solution)/shard_map/all_to_all | solution.py:11
  52.4 1.9 %collective-permute-start = (bf16[4,512,256]{2,1,0:T(8,128)(2,1)S(1)}, bf16[4,512,256]{2,1,0:T(8,128)(2,1)}, u32[]{:S(2)}, u32[]{:S(2)}) collective-permute-start(bf16[4,512,256]{2,1,0:T(8,128)(2,1)S(1)} %bitcast.32), channel_id=1, source_target_pairs={{0,1},{1,0},{2,3},{3,2},{4,5},{5,4},{6,7},{7,6},{8,9},{9,8},{10,11... | collective-permute-start | bytes 3145736 | tf_op jit(solution)/shard_map/ppermute | solution.py:15
  54.4 1.9 %convolution_convert_fusion.1 = bf16[2048,256]{1,0:T(8,128)(2,1)S(1)} fusion(bf16[256,2048]{0,1:T(8,128)(2,1)} %collective-permute-done.1, bf16[256,2048]{0,1:T(8,128)(2,1)S(1)} %bitcast.34, bf16[256,256]{1,0:T(8,128)(2,1)S(1)} %collective-permute-done.2, bf16[256,256]{1,0:T(8,128)(2,1)S(1)} %copy-done.1), kind=kOutput, calls=%fused_computation.2 | convolution fusion | flops 542113792 | bytes 3407872 | tf_op jit(solution)/shard_map/dot_general | solution.py:40
  56.3 1.0 %copy.22 = bf16[4,4,128,256]{3,2,0,1:T(8,128)(2,1)} copy(bf16[4,4,128,256]{3,2,1,0:T(8,128)(2,1)S(1)} %bitcast.36) | data formatting | bytes 2097152 | tf_op jit(solution)/shard_map/reshape | solution.py:41
  57.3 3.5 %all-to-all-start.2 = ((bf16[4,512,256]{2,1,0:T(8,128)(2,1)}), bf16[4,512,256]{2,1,0:T(8,128)(2,1)S(1)}, u32[]{:S(2)}, u32[]{:S(2)}) async-start(bf16[4,512,256]{2,1,0:T(8,128)(2,1)} %bitcast.15), calls=%async_computation.2 | async-start | bytes 2097152 | tf_op jit(solution)/shard_map/all_to_all | solution.py:11
  60.9 16.0 %all-to-all-done.2 = bf16[4,512,256]{2,1,0:T(8,128)(2,1)S(1)} async-done(((bf16[4,512,256]{2,1,0:T(8,128)(2,1)}), bf16[4,512,256]{2,1,0:T(8,128)(2,1)S(1)}, u32[]{:S(2)}, u32[]{:S(2)}) %all-to-all-start.2) | async-done | bytes 1048608 | tf_op jit(solution)/shard_map/all_to_all | solution.py:11
  76.9 0.9 reduce_sum.21
  77.8 7.2 %all-to-all-start.3 = ((bf16[64,8,256]{2,1,0:T(8,128)(2,1)}), bf16[64,8,256]{2,1,0:T(8,128)(2,1)S(1)}, u32[]{:S(2)}, u32[]{:S(2)}) async-start(bf16[64,8,256]{2,1,0:T(8,128)(2,1)} %bitcast.16), calls=%async_computation.3 | async-start | bytes 524288 | tf_op jit(solution)/shard_map/all_to_all | solution.py:11
  85.0 1.4 %select_bitcast_fusion.1 = (bf16[4,1,512,256]{3,2,0,1:T(8,128)(2,1)S(1)}, bf16[4,1,512,256]{3,2,0,1:T(8,128)(2,1)S(1)}) fusion(bf16[4,512,256]{2,1,0:T(8,128)(2,1)} %collective-permute-done, pred[]{:T(512)S(6)} %eq.4, bf16[4,4,128,256]{3,2,1,0:T(8,128)(2,1)S(1)} %copy.19), kind=kLoop, calls=%fused_computation.10 | loop fusion | flops 1048576 | bytes 4194305 | tf_op jit(solution)/shard_map/stack | solution.py:47
  86.7 2.1 %fusion = bf16[256,4096]{0,1:T(8,128)(2,1)} fusion(bf16[4096,256]{1,0:T(8,128)(2,1)S(1)} %bitcast.29, bf16[256,256]{1,0:T(8,128)(2,1)S(1)} %copy-done.1), kind=kOutput, calls=%fused_computation.1 | convolution fusion | flops 537919488 | bytes 4325376 | tf_op jit(solution)/shard_map/dot_general | solution.py:49
  88.8 4.1 %copy.24 = bf16[256,4096]{1,0:T(8,128)(2,1)} copy(bf16[256,4096]{0,1:T(8,128)(2,1)} %fusion) | data formatting | bytes 4194304
  92.9 2.4 %fusion.4 = bf16[256,256]{0,1:T(8,128)(2,1)S(1)} fusion(bf16[4096,256]{1,0:T(8,128)(2,1)S(1)} %bitcast.30, bf16[256,4096]{1,0:T(8,128)(2,1)} %param.4), kind=kOutput, calls=%fused_computation.8 | convolution fusion | flops 536936448 | bytes 4325376 | tf_op jit(solution)/shard_map/dot_general | solution.py:48
  95.2 0.8 copy.23
  96.0 3.1 %all-to-all-done.3 = bf16[64,8,256]{2,1,0:T(8,128)(2,1)S(1)} async-done(((bf16[64,8,256]{2,1,0:T(8,128)(2,1)}), bf16[64,8,256]{2,1,0:T(8,128)(2,1)S(1)}, u32[]{:S(2)}, u32[]{:S(2)}) %all-to-all-start.3) | async-done | bytes 262176 | tf_op jit(solution)/shard_map/all_to_all | solution.py:11
  (12 shorter events, 1.8 us)
Async XLA Ops:
  0.6 0.7 copy-start
  2.7 30.9 %all-to-all-start = ((bf16[64,8,256]{2,1,0:T(8,128)(2,1)}), bf16[64,8,256]{2,1,0:T(8,128)(2,1)S(1)}, u32[]{:S(2)}, u32[]{:S(2)}) async-start(bf16[64,8,256]{2,1,0:T(8,128)(2,1)} %broadcast_in_dim.6), calls=%async_computation | async-start | bytes 524288 | tf_op jit(solution)/shard_map/all_to_all | solution.py:11
  23.8 15.1 %copy-start.1 = (bf16[256,256]{1,0:T(8,128)(2,1)S(1)}, bf16[256,256]{1,0:T(8,128)(2,1)}, u32[]{:S(2)}) copy-start(bf16[256,256]{1,0:T(8,128)(2,1)} %param.7) | copy-start | bytes 393220
  23.8 30.6 %collective-permute-start.1 = (bf16[256,2048]{0,1:T(8,128)(2,1)}, bf16[256,2048]{0,1:T(8,128)(2,1)}, u32[]{:S(2)}, u32[]{:S(2)}) collective-permute-start(bf16[256,2048]{0,1:T(8,128)(2,1)} %bitcast.12), channel_id=1, source_target_pairs={{0,1},{1,0},{2,3},{3,2},{4,5},{5,4},{6,7},{7,6},{8,9},{9,8},{10,11... | collective-permute-start | bytes 3145736 | tf_op jit(solution)/shard_map/ppermute | solution.py:15
  34.6 17.7 %all-to-all-start.1 = ((bf16[4,512,256]{2,1,0:T(8,128)(2,1)}), bf16[4,512,256]{2,1,0:T(8,128)(2,1)S(1)}, u32[]{:S(2)}, u32[]{:S(2)}) async-start(bf16[4,512,256]{2,1,0:T(8,128)(2,1)} %broadcast_in_dim.15), calls=%async_computation.1 | async-start | bytes 2097152 | tf_op jit(solution)/shard_map/all_to_all | solution.py:11
  38.9 15.4 %collective-permute-start.2 = (bf16[256,256]{1,0:T(8,128)(2,1)S(1)}, bf16[256,256]{1,0:T(8,128)(2,1)S(1)}, u32[]{:S(2)}, u32[]{:S(2)}) collective-permute-start(bf16[256,256]{1,0:T(8,128)(2,1)S(1)} %copy-done.1), channel_id=1, source_target_pairs={{0,1},{1,0},{2,3},{3,2},{4,5},{5,4},{6,7},{7,6},{8,9},{9,8},{10,11... | collective-permute-start | bytes 393224 | tf_op jit(solution)/shard_map/ppermute | solution.py:15
  52.4 32.6 %collective-permute-start = (bf16[4,512,256]{2,1,0:T(8,128)(2,1)S(1)}, bf16[4,512,256]{2,1,0:T(8,128)(2,1)}, u32[]{:S(2)}, u32[]{:S(2)}) collective-permute-start(bf16[4,512,256]{2,1,0:T(8,128)(2,1)S(1)} %bitcast.32), channel_id=1, source_target_pairs={{0,1},{1,0},{2,3},{3,2},{4,5},{5,4},{6,7},{7,6},{8,9},{9,8},{10,11... | collective-permute-start | bytes 3145736 | tf_op jit(solution)/shard_map/ppermute | solution.py:15
  57.3 19.5 %all-to-all-start.2 = ((bf16[4,512,256]{2,1,0:T(8,128)(2,1)}), bf16[4,512,256]{2,1,0:T(8,128)(2,1)S(1)}, u32[]{:S(2)}, u32[]{:S(2)}) async-start(bf16[4,512,256]{2,1,0:T(8,128)(2,1)} %bitcast.15), calls=%async_computation.2 | async-start | bytes 2097152 | tf_op jit(solution)/shard_map/all_to_all | solution.py:11
  77.8 21.4 %all-to-all-start.3 = ((bf16[64,8,256]{2,1,0:T(8,128)(2,1)}), bf16[64,8,256]{2,1,0:T(8,128)(2,1)S(1)}, u32[]{:S(2)}, u32[]{:S(2)}) async-start(bf16[64,8,256]{2,1,0:T(8,128)(2,1)} %bitcast.16), calls=%async_computation.3 | async-start | bytes 524288 | tf_op jit(solution)/shard_map/all_to_all | solution.py:11

commit v2 on v1

v2 whole, which is shorter than its diff:
```python
import functools

import jax
import jax.numpy as jnp
from jax import lax
from jax.experimental import pallas as pl
from jax.experimental.pallas import tpu as pltpu
from jax.sharding import Mesh, PartitionSpec as P

BLOCK = 2048
TORUS = ("yl", "yh", "z")
VMEM_BYTES = 32 * 1024 * 1024
F32, BF16 = jnp.float32, jnp.bfloat16
ANY = pl.BlockSpec(memory_space=pl.ANY)
VMEM = pl.BlockSpec(memory_space=pltpu.VMEM)


def exchange(pieces, axis):
    return lax.all_to_all(pieces, axis, 0, 0, tiled=True)


def swap(value):
    return lax.ppermute(value, "c", [(0, 1), (1, 0)])


def call(kernel, out_shape, in_specs, out_specs, scratch, flops, moved, aliases=None):
    return pl.pallas_call(
        kernel,
        out_shape=out_shape,
        in_specs=in_specs,
        out_specs=out_specs,
        scratch_shapes=scratch,
        input_output_aliases=aliases or {},
        compiler_params=pltpu.CompilerParams(vmem_limit_bytes=VMEM_BYTES),
        cost_estimate=pl.CostEstimate(flops=flops, bytes_accessed=moved, transcendentals=0),
    )


def columns(part, core, share):
    return pl.ds(pl.multiple_of((part * 2 + core) * share, share), share)


def prepare(hidden, codes, scales, cotangent, copies, give, sems):
    tokens, width = hidden.shape
    share = width // 8
    other = 1 - lax.axis_index("c")
    sends = []
    for part in range(4):
        sends.append(
            pltpu.make_async_copy(
                hidden.at[:, columns(part, other, share)],
                give.at[:, pl.ds(part * share, share)],
                sems.at[part],
            )
        )
    sends.append(pltpu.make_async_copy(cotangent, give.at[:, pl.ds(4 * share, cotangent.shape[1])], sems.at[4]))
    for send in sends:
        send.start()
    scale = jnp.where(lax.axis_index("yl") * (2 * share) >= BLOCK, scales[1:2, :], scales[0:1, :])
    own = (codes[...].astype(F32) * scale).astype(BF16)
    twice = jnp.concatenate([own, own], axis=0)
    for at in range(0, copies.shape[0], 16):
        copies[at : at + 16, :] = twice
    for send in sends:
        send.wait()


def pair_terms(hidden, cotangent, got, term, own_cols, got_cols, own_cot, got_cot, out, load_sems, cot_sems, out_sems):
    tokens, width = hidden.shape
    share = width // 8
    core = lax.axis_index("c")
    cots = [
        pltpu.make_async_copy(cotangent, own_cot, cot_sems.at[0]),
        pltpu.make_async_copy(got.at[:, pl.ds(4 * share, cotangent.shape[1])], got_cot, cot_sems.at[1]),
    ]
    loads = []
    for part in range(4):
        loads.append(
            (
                pltpu.make_async_copy(
                    hidden.at[:, columns(part, core, share)], own_cols.at[part], load_sems.at[part, 0]
                ),
                pltpu.make_async_copy(
                    got.at[:, pl.ds(part * share, share)], got_cols.at[part], load_sems.at[part, 1]
                ),
            )
        )
    for copy in cots:
        copy.start()
    for pair in loads:
        for copy in pair:
            copy.start()
    for copy in cots:
        copy.wait()
    stores = []
    dims = (((0,), (0,)), ((), ()))
    for part in range(4):
        for copy in loads[part]:
            copy.wait()
        total = lax.dot_general(own_cols[part], own_cot[...], dims, preferred_element_type=F32)
        total += lax.dot_general(got_cols[part], got_cot[...], dims, preferred_element_type=F32)
        out[:, part] = total.astype(BF16).reshape(out.shape[0], out.shape[2], out.shape[3])
        store = pltpu.make_async_copy(out.at[:, part], term.at[:, part], out_sems.at[part])
        store.start()
        stores.append(store)
    for store in stores:
        store.wait()


def weight_half(which, hidden, cotangent, weight, *rest):
    if which == 0:
        acc_out, grad, cols, pieces, cot, out, load_sems, cot_sem, out_sems = rest
    else:
        acc_in, grad_in, acc_out, grad, cols, pieces, cot, out, load_sems, cot_sem, out_sems = rest
    tokens, width = hidden.shape
    share = width // 8
    core = lax.axis_index("c")
    if which == 1:
        core = 1 - core
    cot_load = pltpu.make_async_copy(cotangent, cot, cot_sem.at[0])
    loads = []
    for part in range(4):
        loads.append(
            (
                pltpu.make_async_copy(weight.at[:, part], pieces.at[part], load_sems.at[part, 0]),
                pltpu.make_async_copy(hidden.at[:, columns(part, core, share)], cols.at[part], load_sems.at[part, 1]),
            )
        )
    cot_load.start()
    for pair in loads:
        for copy in pair:
            copy.start()
    cot_load.wait()
    stores = []
    if which == 0:
        total = jnp.zeros(acc_out.shape, F32)
    else:
        total = acc_in[...]
    for part in range(4):
        for copy in loads[part]:
            copy.wait()
        rows = pieces[part].reshape(share, weight.shape[3])
        out[part] = lax.dot_general(
            cot[...], rows, (((1,), (1,)), ((), ())), preferred_element_type=F32
        ).astype(BF16)
        store = pltpu.make_async_copy(out.at[part], grad.at[:, columns(part, core, share)], out_sems.at[part])
        store.start()
        stores.append(store)
        total += jnp.dot(cols[part], rows, preferred_element_type=F32)
    acc_out[...] = total.astype(acc_out.dtype)
    for store in stores:
        store.wait()


def body(hidden, codes, scales, cotangent):
    tokens, width = hidden.shape
    rows, cols = codes.shape
    share = width // 8
    piece = share // 4
    dma = pltpu.SemaphoreType.DMA
    sds = jax.ShapeDtypeStruct
    half_flops = 2 * tokens * (width // 2) * cols

    copies, give = call(
        prepare,
        (sds((64 * rows, cols), BF16), sds((tokens, width // 2 + cols), BF16)),
        [ANY, VMEM, VMEM, ANY],
        (VMEM, ANY),
        [dma((5,))],
        0,
        3 << 20,
    )(hidden, codes, scales, cotangent)
    got = swap(give)
    plane = exchange(copies.reshape(64, rows, cols), TORUS)

    term = call(
        pair_terms,
        sds((4, 4, piece, cols), BF16),
        [ANY, ANY, ANY],
        ANY,
        [
            pltpu.VMEM((4, tokens, share), BF16),
            pltpu.VMEM((4, tokens, share), BF16),
            pltpu.VMEM((tokens, cols), BF16),
            pltpu.VMEM((tokens, cols), BF16),
            pltpu.VMEM((4, 4, piece, cols), BF16),
            dma((4, 2)),
            dma((2,)),
            dma((4,)),
        ],
        2 * half_flops,
        4 << 20,
    )(hidden, cotangent, got)
    sums = exchange(term.reshape(4, 4 * piece, cols), "x")

    plane, term = lax.optimization_barrier((plane, term))
    half = exchange(jnp.broadcast_to(plane.reshape(1, 4 * piece, cols), (4, 4 * piece, cols)), "x")
    half = half.reshape(4, 4, piece, cols)
    other = swap(half)

    sums = jnp.sum(sums.astype(F32), axis=0).astype(BF16)
    grad_weight = jnp.sum(exchange(sums.reshape(64, rows, cols), TORUS).astype(F32), axis=0)

    scratch = [
        pltpu.VMEM((4, tokens, share), BF16),
        pltpu.VMEM((4, 4, piece, cols), BF16),
        pltpu.VMEM((tokens, cols), BF16),
        pltpu.VMEM((4, tokens, share), BF16),
        dma((4, 2)),
        dma((1,)),
        dma((4,)),
    ]
    part, grad = call(
        functools.partial(weight_half, 0),
        (sds((tokens, cols), F32), sds((tokens, width), BF16)),
        [ANY, ANY, ANY],
        (VMEM, ANY),
        scratch,
        2 * half_flops,
        4 << 20,
    )(hidden, cotangent, half)
    projected, grad_hidden = call(
        functools.partial(weight_half, 1),
        (sds((tokens, cols), BF16), sds((tokens, width), BF16)),
        [ANY, ANY, ANY, VMEM, ANY],
        (VMEM, ANY),
        scratch,
        2 * half_flops,
        4 << 20,
        {4: 1},
    )(hidden, cotangent, other, part, grad)
    return projected, grad_hidden, grad_weight


def solution(mesh):
    fine = Mesh(mesh.devices.reshape(4, 2, 8, 4, 2), ("x", "yh", "z", "yl", "c"))
    outer, node = ("x", "yh", "z"), ("yl", "c")
    tokens, rows = P(outer + node, None), P(node + outer, None)
    return jax.shard_map(
        body,
        mesh=fine,
        in_specs=(tokens, rows, P(), tokens),
        out_specs=(tokens, tokens, rows),
        check_vma=False,
    )
```

time: 101 us -> 103 us (1.020)
  blocking collectives: 0 us -> 18 us
  Pallas kernels: 0 us -> 11.3 us
  local copies, waits for them, and re-layouts: 13 us -> 4.9 us
  waiting for transfers between devices: 38.4 us -> 31.9 us
  matrix products: 6.37 us -> 0 us
  starting transfers between devices: 37.5 us -> 32.2 us
    all_to_all x0 -> x1, blocking collectives: none -> 18 us  [exchange(): return lax.all_to_all(pieces, axis, 0, 0, tiled=True)]
    pallas_call x0 -> x4, Pallas kernels: none -> 11.3 us  [the longest x1 3.85 us: body(): call(functools.partial(weight_half, 1), (sds((tokens, cols), BF16), sds((...]
    all_to_all x4 -> x3, waiting for transfers between devices: 38.3 us -> 31.9 us  [exchange(): return lax.all_to_all(pieces, axis, 0, 0, tiled=True)]
    dot_general x3 -> x0, matrix products: 6.37 us -> none  [the longest x1 2.37 us: body(): projected = jnp.dot(hidden, whole, preferred_element_type=f32).astype(bf16)]
    unnamed x7 -> x14, local copies, waits for them, and re-layouts: 8.76 us -> 4.83 us
    all_to_all x4 -> x3, starting transfers between devices: 31.6 us -> 28.3 us  [exchange(): return lax.all_to_all(pieces, axis, 0, 0, tiled=True)]
    reduce_sum x2, other arithmetic: 1.57 us -> 3.75 us  [the longest x1 2.13 us: body(): sums = jnp.sum(sums.astype(F32), axis=0).astype(BF16)]
    ppermute x3 -> x2, starting transfers between devices: 5.87 us -> 3.84 us  [swap(): return lax.ppermute(value, 'c', [(0, 1), (1, 0)])]
  transfers between devices with their start and end apart: 7 -> 5, of which waited for: 4 -> 3; matrix products, arithmetic and copies ran while one was open for 20% -> 4% of each run, Pallas kernels for 0% -> 6%
where the time goes in v2:
time: 103 us
  starting transfers between devices  32.2 us (31%)
  waiting for transfers between devices  31.9 us (31%)
  blocking collectives  18 us (17%)
  Pallas kernels  11.3 us (11%)
  local copies, waits for them, and re-layouts  4.9 us (5%)
  other arithmetic  3.75 us (4%)
    all_to_all x3, waiting for transfers between devices, exchange(): return lax.all_to_all(pieces, axis, 0, 0, tiled=True)  31.9 us
    all_to_all x3, starting transfers between devices, exchange(): return lax.all_to_all(pieces, axis, 0, 0, tiled=True)  28.3 us
    all_to_all x1, blocking collectives, exchange(): return lax.all_to_all(pieces, axis, 0, 0, tiled=True)  18 us
    unnamed x14, local copies, waits for them, and re-layouts  4.83 us
    pallas_call x1, Pallas kernels, body(): call(functools.partial(weight_half, 1), (sds((tokens, cols), BF16), sds((...  3.85 us
    ppermute x2, starting transfers between devices, swap(): return lax.ppermute(value, 'c', [(0, 1), (1, 0)])  3.84 us
    pallas_call x1, Pallas kernels, body(): call(pair_terms, sds((4, 4, piece, cols), BF16), [ANY, ANY, ANY], ANY, [p...  3.19 us
    pallas_call x1, Pallas kernels, body(): call(functools.partial(weight_half, 0), (sds((tokens, cols), F32), sds((t...  2.47 us
  transfers between devices with their start and end apart: 5, of which 3 were waited for; matrix products, arithmetic and copies ran while one was open for 4% of the time, Pallas kernels for 6%

profile of v2, /device:TPU:8, one launch (start us, length us, event | category | flops | bytes accessed | tf_op | source)
XLA Modules:
  0.0 102.7 jit_solution(8528180589668495146)
XLA Ops:
  0.6 1.6 %copy-done = bf16[256,4096]{1,0:T(8,128)(2,1)S(1)} copy-done((bf16[256,4096]{1,0:T(8,128)(2,1)S(1)}, bf16[256,4096]{1,0:T(8,128)(2,1)}, u32[]{:S(2)}) %copy-start) | copy-done | bytes 2097176
  2.2 0.9 copy-done.3
  3.1 0.7 copy-done.5
  3.8 0.7 copy-done.6
  4.5 1.8 %shard_map.67 = (bf16[512,256]{1,0:T(8,128)(2,1)}, bf16[256,2304]{1,0:T(8,128)(2,1)}) custom-call(bf16[256,4096]{1,0:T(8,128)(2,1)S(1)} %copy-done, bf16[8,256]{1,0:T(8,128)(2,1)S(1)} %copy-done.5, f32[2,256]{1,0:T(2,128)S(1)} %copy-done.6, bf16[256,256]{1,0:T(8,128)(2,1)S(1)} %copy-done.3), custom_call_target="tpu_custom_call" | custom-call | bytes 3145728 | tf_op jit(solution)/shard_map/pallas_call | solution.py:164
  6.3 1.9 %collective-permute-start = (bf16[256,2304]{1,0:T(8,128)(2,1)}, bf16[256,2304]{1,0:T(8,128)(2,1)}, u32[]{:S(2)}, u32[]{:S(2)}) collective-permute-start(bf16[256,2304]{1,0:T(8,128)(2,1)} %get-tuple-element.11), channel_id=1, source_target_pairs={{0,1},{1,0},{2,3},{3,2},{4,5},{5,4},{6,7},{7,6},{8,9},{9,8},{10,11... | collective-permute-start | bytes 3538952 | tf_op jit(solution)/shard_map/ppermute | solution.py:23
  8.2 16.6 %all-to-all-start = ((bf16[64,8,256]{2,1,0:T(8,128)(2,1)}), bf16[64,8,256]{2,1,0:T(8,128)(2,1)S(1)}, u32[]{:S(2)}, u32[]{:S(2)}) async-start(bf16[64,8,256]{2,1,0:T(8,128)(2,1)} %bitcast), calls=%async_computation | async-start | bytes 524288 | tf_op jit(solution)/shard_map/all_to_all | solution.py:19
  24.8 0.0 collective-permute-done.got
  24.8 3.2 %shard_map.68 = bf16[4,4,128,256]{3,2,1,0:T(8,128)(2,1)S(1)} custom-call(bf16[256,4096]{1,0:T(8,128)(2,1)S(1)} %copy-done.1, bf16[256,256]{1,0:T(8,128)(2,1)S(1)} %copy-done.4, bf16[256,2304]{1,0:T(8,128)(2,1)} %collective-permute-done.got), custom_call_target="tpu_custom_call" | custom-call | flops 536870912 | bytes 4194304 | tf_op jit(solution)/shard_map/pallas_call | solution.py:176
  28.0 0.0 copy-start.2
  28.0 1.0 copy-done.2
  29.0 10.7 %all-to-all-done = bf16[64,8,256]{2,1,0:T(8,128)(2,1)S(1)} async-done(((bf16[64,8,256]{2,1,0:T(8,128)(2,1)}), bf16[64,8,256]{2,1,0:T(8,128)(2,1)S(1)}, u32[]{:S(2)}, u32[]{:S(2)}) %all-to-all-start) | async-done | bytes 262176 | tf_op jit(solution)/shard_map/all_to_all | solution.py:19
  39.7 0.1 broadcast_in_dim.8
  39.8 18.0 %all_to_all.20 = bf16[4,512,256]{2,1,0:T(8,128)(2,1)S(1)} all-to-all(bf16[4,512,256]{2,1,0:T(8,128)(2,1)S(1)} %broadcast_in_dim.8), channel_id=1, replica_groups=mesh['x'=4,'yh'=2,'z'=8,'yl'=4,'c'=2] {'x'}, dimensions={0} | all-to-all | bytes 2097152 | tf_op jit(solution)/shard_map/all_to_all | solution.py:19
  57.8 4.3 %all-to-all-start.2 = ((bf16[4,512,256]{2,1,0:T(8,128)(2,1)}), bf16[4,512,256]{2,1,0:T(8,128)(2,1)}, u32[]{:S(2)}, u32[]{:S(2)}) async-start(bf16[4,512,256]{2,1,0:T(8,128)(2,1)} %bitcast.7), calls=%async_computation.2 | async-start | bytes 2097152 | tf_op jit(solution)/shard_map/all_to_all | solution.py:19
  62.1 1.9 %collective-permute-start.1 = (bf16[4,4,128,256]{3,2,1,0:T(8,128)(2,1)S(1)}, bf16[4,4,128,256]{3,2,1,0:T(8,128)(2,1)}, u32[]{:S(2)}, u32[]{:S(2)}) collective-permute-start(bf16[4,4,128,256]{3,2,1,0:T(8,128)(2,1)S(1)} %bitcast.5), channel_id=1, source_target_pairs={{0,1},{1,0},{2,3},{3,2},{4,5},{5,4},{6,7},{7,6},{8,9},{9,8},{10,11... | collective-permute-start | bytes 3145736 | tf_op jit(solution)/shard_map/ppermute | solution.py:23
  64.0 10.8 %all-to-all-done.2 = bf16[4,512,256]{2,1,0:T(8,128)(2,1)} async-done(((bf16[4,512,256]{2,1,0:T(8,128)(2,1)}), bf16[4,512,256]{2,1,0:T(8,128)(2,1)}, u32[]{:S(2)}, u32[]{:S(2)}) %all-to-all-start.2) | async-done | bytes 1048608 | tf_op jit(solution)/shard_map/all_to_all | solution.py:19
  74.8 2.1 %reduce_sum.21 = bf16[512,256]{1,0:T(8,128)(2,1)} reduce(bf16[4,512,256]{2,1,0:T(8,128)(2,1)} %all-to-all-done.2, bf16[]{:T(256)} %constant.2.clone.1), dimensions={0}, to_apply=%region_0.0 | reduce | flops 393216 | bytes 1310722 | tf_op jit(solution)/shard_map/reduce_sum | solution.py:201
  77.0 7.5 %all-to-all-start.3 = ((bf16[64,8,256]{2,1,0:T(8,128)(2,1)}), bf16[64,8,256]{2,1,0:T(8,128)(2,1)}, u32[]{:S(2)}, u32[]{:S(2)}) async-start(bf16[64,8,256]{2,1,0:T(8,128)(2,1)} %bitcast.4), calls=%async_computation.3 | async-start | bytes 524288 | tf_op jit(solution)/shard_map/all_to_all | solution.py:19
  84.4 2.5 %shard_map.69 = (f32[256,256]{1,0:T(8,128)S(1)}, bf16[256,4096]{1,0:T(8,128)(2,1)}) custom-call(bf16[256,4096]{1,0:T(8,128)(2,1)S(1)} %copy-done.1, bf16[256,256]{1,0:T(8,128)(2,1)S(1)} %copy-done.4, bf16[4,4,128,256]{3,2,1,0:T(8,128)(2,1)S(1)} %bitcast.6), custom_call_target="tpu_custom_call" | custom-call | flops 536870912 | bytes 4194304 | tf_op jit(solution)/shard_map/pallas_call | solution.py:213
  86.9 10.3 %all-to-all-done.3 = bf16[64,8,256]{2,1,0:T(8,128)(2,1)} async-done(((bf16[64,8,256]{2,1,0:T(8,128)(2,1)}), bf16[64,8,256]{2,1,0:T(8,128)(2,1)}, u32[]{:S(2)}, u32[]{:S(2)}) %all-to-all-start.3) | async-done | bytes 262176 | tf_op jit(solution)/shard_map/all_to_all | solution.py:19
  97.3 1.6 %convert_reduce_fusion = f32[8,256]{1,0:T(8,128)} fusion(bf16[64,8,256]{2,1,0:T(8,128)(2,1)} %all-to-all-done.3), kind=kLoop, calls=%fused_computation | loop fusion | flops 260096 | bytes 270336 | tf_op jit(solution)/shard_map/reduce_sum | solution.py:202
  98.9 0.0 collective-permute-done.1.weight
  98.9 3.9 %shard_map.70 = (bf16[256,256]{1,0:T(8,128)(2,1)}, bf16[256,4096]{1,0:T(8,128)(2,1)}) custom-call(bf16[256,4096]{1,0:T(8,128)(2,1)S(1)} %copy-done.1, bf16[256,256]{1,0:T(8,128)(2,1)S(1)} %copy-done.4, bf16[4,4,128,256]{3,2,1,0:T(8,128)(2,1)} %collective-permute-done.1.weight, ...), custom_call_target="tpu_custom_call", output_to_operand_aliasing={{1}: (4, {})} | custom-call | flops 536870912 | bytes 4194304 | tf_op jit(solution)/shard_map/pallas_call | solution.py:222
  (8 shorter events, 0.0 us)
Async XLA Ops:
  0.6 1.6 %copy-start = (bf16[256,4096]{1,0:T(8,128)(2,1)S(1)}, bf16[256,4096]{1,0:T(8,128)(2,1)}, u32[]{:S(2)}) copy-start(bf16[256,4096]{1,0:T(8,128)(2,1)} %hidden.7) | copy-start | bytes 6291460
  2.2 0.9 copy-start.3
  3.1 0.7 copy-start.5
  3.8 0.7 copy-start.6
  4.5 20.3 %copy-start.1 = (bf16[256,4096]{1,0:T(8,128)(2,1)S(1)}, bf16[256,4096]{1,0:T(8,128)(2,1)}, u32[]{:S(2)}) copy-start(bf16[256,4096]{1,0:T(8,128)(2,1)} %hidden.7) | copy-start | bytes 6291460
  4.5 20.3 %copy-start.4 = (bf16[256,256]{1,0:T(8,128)(2,1)S(1)}, bf16[256,256]{1,0:T(8,128)(2,1)}, u32[]{:S(2)}) copy-start(bf16[256,256]{1,0:T(8,128)(2,1)} %cotangent.7) | copy-start | bytes 393220
  6.3 18.5 %collective-permute-start = (bf16[256,2304]{1,0:T(8,128)(2,1)}, bf16[256,2304]{1,0:T(8,128)(2,1)}, u32[]{:S(2)}, u32[]{:S(2)}) collective-permute-start(bf16[256,2304]{1,0:T(8,128)(2,1)} %get-tuple-element.11), channel_id=1, source_target_pairs={{0,1},{1,0},{2,3},{3,2},{4,5},{5,4},{6,7},{7,6},{8,9},{9,8},{10,11... | collective-permute-start | bytes 3538952 | tf_op jit(solution)/shard_map/ppermute | solution.py:23
  8.2 31.5 %all-to-all-start = ((bf16[64,8,256]{2,1,0:T(8,128)(2,1)}), bf16[64,8,256]{2,1,0:T(8,128)(2,1)S(1)}, u32[]{:S(2)}, u32[]{:S(2)}) async-start(bf16[64,8,256]{2,1,0:T(8,128)(2,1)} %bitcast), calls=%async_computation | async-start | bytes 524288 | tf_op jit(solution)/shard_map/all_to_all | solution.py:19
  28.0 1.0 copy-start.2
  57.8 17.0 %all-to-all-start.2 = ((bf16[4,512,256]{2,1,0:T(8,128)(2,1)}), bf16[4,512,256]{2,1,0:T(8,128)(2,1)}, u32[]{:S(2)}, u32[]{:S(2)}) async-start(bf16[4,512,256]{2,1,0:T(8,128)(2,1)} %bitcast.7), calls=%async_computation.2 | async-start | bytes 2097152 | tf_op jit(solution)/shard_map/all_to_all | solution.py:19
  62.1 36.8 %collective-permute-start.1 = (bf16[4,4,128,256]{3,2,1,0:T(8,128)(2,1)S(1)}, bf16[4,4,128,256]{3,2,1,0:T(8,128)(2,1)}, u32[]{:S(2)}, u32[]{:S(2)}) collective-permute-start(bf16[4,4,128,256]{3,2,1,0:T(8,128)(2,1)S(1)} %bitcast.5), channel_id=1, source_target_pairs={{0,1},{1,0},{2,3},{3,2},{4,5},{5,4},{6,7},{7,6},{8,9},{9,8},{10,11... | collective-permute-start | bytes 3145736 | tf_op jit(solution)/shard_map/ppermute | solution.py:23
  77.0 20.3 %all-to-all-start.3 = ((bf16[64,8,256]{2,1,0:T(8,128)(2,1)}), bf16[64,8,256]{2,1,0:T(8,128)(2,1)}, u32[]{:S(2)}, u32[]{:S(2)}) async-start(bf16[64,8,256]{2,1,0:T(8,128)(2,1)} %bitcast.4), calls=%async_computation.3 | async-start | bytes 524288 | tf_op jit(solution)/shard_map/all_to_all | solution.py:19

commit v3 on v1

v3 whole, which is shorter than its diff:
```python
import functools

import jax
import jax.numpy as jnp
from jax import lax
from jax.experimental import pallas as pl
from jax.experimental.pallas import tpu as pltpu
from jax.sharding import Mesh, PartitionSpec as P

BLOCK = 2048
TORUS = ("yh", "z", "yl")
VMEM_BYTES = 32 * 1024 * 1024
F32, BF16 = jnp.float32, jnp.bfloat16
HBM = pl.BlockSpec(memory_space=pltpu.HBM)
ANY = pl.BlockSpec(memory_space=pl.ANY)
VMEM = pl.BlockSpec(memory_space=pltpu.VMEM)


def exchange(pieces):
    return lax.all_to_all(pieces, TORUS, 0, 0, tiled=True)


def swap(value):
    return lax.ppermute(value, "c", [(0, 1), (1, 0)])


def along_x(value, shift):
    return lax.ppermute(value, "x", [(at, (at + shift) % 4) for at in range(4)])


def call(kernel, out_shape, in_specs, out_specs, scratch, flops, moved, aliases=None, limit=VMEM_BYTES):
    return pl.pallas_call(
        kernel,
        out_shape=out_shape,
        in_specs=in_specs,
        out_specs=out_specs,
        scratch_shapes=scratch,
        input_output_aliases=aliases or {},
        compiler_params=pltpu.CompilerParams(vmem_limit_bytes=limit),
        cost_estimate=pl.CostEstimate(flops=flops, bytes_accessed=moved, transcendentals=0),
    )


def columns(part, core, share):
    return pl.ds(pl.multiple_of((part * 2 + core) * share, share), share)


def prepare(hidden, codes, scales, cotangent, copies, give, code_buf, scale_buf, copy_buf, give_buf, load_sems, store_sems):
    width = hidden.shape[1]
    share = width // 8
    other = 1 - lax.axis_index("c")
    edge = pl.ds(4 * share, cotangent.shape[1])
    loads, stores = [], []
    for part in range(4):
        slot = pl.ds(part * share, share)
        loads.append(
            pltpu.make_async_copy(hidden.at[:, columns(part, other, share)], give_buf.at[:, slot], load_sems.at[part])
        )
        stores.append(pltpu.make_async_copy(give_buf.at[:, slot], give.at[:, slot], store_sems.at[part]))
    loads.append(pltpu.make_async_copy(cotangent, give_buf.at[:, edge], load_sems.at[4]))
    stores.append(pltpu.make_async_copy(give_buf.at[:, edge], give.at[:, edge], store_sems.at[4]))
    small = [
        pltpu.make_async_copy(codes, code_buf, load_sems.at[5]),
        pltpu.make_async_copy(scales, scale_buf, load_sems.at[6]),
    ]
    for copy in small + loads:
        copy.start()
    for copy in small:
        copy.wait()
    scale = jnp.where(lax.axis_index("yl") * (2 * share) >= BLOCK, scale_buf[1:2, :], scale_buf[0:1, :])
    own = (code_buf[...].astype(F32) * scale).astype(BF16)
    twice = jnp.concatenate([own, own], axis=0)
    for at in range(0, copies.shape[0], 16):
        copy_buf[at : at + 16, :] = twice
    stores.append(pltpu.make_async_copy(copy_buf, copies, store_sems.at[5]))
    stores[5].start()
    for load, store in zip(loads, stores):
        load.wait()
        store.start()
    for store in stores:
        store.wait()


def pair_terms(hidden, cotangent, got, term0, term1, term2, term3, outs, sems):
    share = hidden.shape[1] // 8
    piece = share // 4
    core, me = lax.axis_index("c"), lax.axis_index("x")
    dims = (((0,), (0,)), ((), ()))
    got_cot = got[:, 4 * share :]
    stores = []
    for shift, term in ((2, term2), (1, term1), (3, term3), (0, term0)):
        at = lax.rem(me + shift, 4) * piece
        for part in range(4):
            mine = pl.ds(pl.multiple_of((part * 2 + core) * share + at, piece), piece)
            theirs = pl.ds(pl.multiple_of(part * share + at, piece), piece)
            total = lax.dot_general(hidden[:, mine], cotangent[...], dims, preferred_element_type=F32)
            total += lax.dot_general(got[:, theirs], got_cot, dims, preferred_element_type=F32)
            outs[shift, :, part] = total.astype(BF16).reshape(outs.shape[1], outs.shape[3], outs.shape[4])
        store = pltpu.make_async_copy(outs.at[shift], term, sems.at[shift])
        store.start()
        stores.append(store)
    for store in stores:
        store.wait()


def assemble(piece0, piece1, piece2, piece3, rows):
    me = lax.axis_index("x")
    blocks, _, height, _ = piece0.shape
    for shift, source in enumerate((piece0, piece1, piece2, piece3)):
        at = lax.rem(me + 4 - shift, 4) * (blocks * height)
        for part in range(4):
            for block in range(0, blocks, 2):
                start = pl.multiple_of(at + block * height, 2 * height)
                rows[part, pl.ds(start, 2 * height), :] = jnp.concatenate(
                    [source[block, part], source[block + 1, part]], axis=0
                )


def weight_half(which, hidden, cotangent, rows, *rest):
    if which == 0:
        acc_out, grad, out, out_sems = rest
        total = jnp.zeros(acc_out.shape, F32)
    else:
        acc_in, grad_in, acc_out, grad, out, out_sems = rest
        total = acc_in[...]
    share = hidden.shape[1] // 8
    core = lax.axis_index("c")
    if which == 1:
        core = 1 - core
    stores = []
    for part in range(4):
        out[part] = lax.dot_general(
            cotangent[...], rows[part], (((1,), (1,)), ((), ())), preferred_element_type=F32
        ).astype(BF16)
        store = pltpu.make_async_copy(out.at[part], grad.at[:, columns(part, core, share)], out_sems.at[part])
        store.start()
        stores.append(store)
        total += jnp.dot(hidden[:, columns(part, core, share)], rows[part], preferred_element_type=F32)
    acc_out[...] = total.astype(acc_out.dtype)
    for store in stores:
        store.wait()


def body(hidden, codes, scales, cotangent):
    tokens, width = hidden.shape
    rows, cols = codes.shape
    share = width // 8
    piece = share // 4
    dma = pltpu.SemaphoreType.DMA
    sds = jax.ShapeDtypeStruct
    half_flops = 2 * tokens * (width // 2) * cols

    copies, give = call(
        prepare,
        (sds((64 * rows, cols), BF16), sds((tokens, width // 2 + cols), BF16)),
        [HBM, HBM, HBM, HBM],
        (HBM, HBM),
        [
            pltpu.VMEM((rows, cols), BF16),
            pltpu.VMEM((2, cols), F32),
            pltpu.VMEM((64 * rows, cols), BF16),
            pltpu.VMEM((tokens, width // 2 + cols), BF16),
            dma((7,)),
            dma((6,)),
        ],
        0,
        3 << 20,
        limit=61 * 1024 * 1024,
    )(hidden, codes, scales, cotangent)
    got = swap(give)
    plane = exchange(copies.reshape(64, rows, cols))

    terms = call(
        pair_terms,
        [sds((16, 4, rows, cols), BF16)] * 4,
        [VMEM, VMEM, VMEM],
        [HBM] * 4,
        [pltpu.VMEM((4, 16, 4, rows, cols), BF16), dma((4,))],
        2 * half_flops,
        4 << 20,
    )(hidden, cotangent, got)
    t2, t1, t3 = [along_x(terms[shift], shift) for shift in (2, 1, 3)]
    plane, terms = lax.optimization_barrier((plane, terms))
    plane = plane.reshape(16, 4, rows, cols)
    p3, p2, p1 = [along_x(plane, shift) for shift in (3, 2, 1)]
    sums = terms[0].astype(F32)
    for value in (t1, t2, t3):
        sums += value.astype(F32)
    sums = sums.astype(BF16).reshape(64, rows, cols)
    blocks = exchange(sums)
    mine = call(
        assemble,
        sds((4, share, cols), BF16),
        [VMEM] * 4,
        VMEM,
        [],
        0,
        2 << 20,
    )(plane, p1, p2, p3)
    other = swap(mine)

    scratch = [
        pltpu.VMEM((4, tokens, share), BF16),
        dma((4,)),
    ]
    part, grad = call(
        functools.partial(weight_half, 0),
        (sds((tokens, cols), F32), sds((tokens, width), BF16)),
        [VMEM] * 3,
        (VMEM, HBM),
        scratch,
        200 * half_flops,
        4 << 20,
    )(hidden, cotangent, mine)
    projected, grad_hidden = call(
        functools.partial(weight_half, 1),
        (sds((tokens, cols), BF16), sds((tokens, width), BF16)),
        [VMEM] * 4 + [HBM],
        (VMEM, HBM),
        scratch,
        2 * half_flops,
        4 << 20,
        {4: 1},
    )(hidden, cotangent, other, part, grad)
    blocks, projected = lax.optimization_barrier((blocks, projected))
    grad_weight = jnp.sum(blocks.astype(F32), axis=0)
    return projected, grad_hidden, grad_weight


def solution(mesh):
    fine = Mesh(mesh.devices.reshape(4, 2, 8, 4, 2), ("x", "yh", "z", "yl", "c"))
    outer, node = ("x", "yh", "z"), ("yl", "c")
    tokens, rows = P(outer + node, None), P(node + outer, None)
    return jax.shard_map(
        body,
        mesh=fine,
        in_specs=(tokens, rows, P(), tokens),
        out_specs=(tokens, tokens, rows),
        check_vma=False,
    )
```

time: 101 us -> 75.9 us (0.75)
  the two profiles are of different devices: /device:TPU:8 before, /device:TPU:2 now
where the time goes in v3:
time: 75.9 us; the launch traced here: 75.4 us
  starting transfers between devices  51.3 us (68%)
  waiting for transfers between devices  11 us (14%)
  Pallas kernels  9.65 us (13%)
  other arithmetic  2.59 us (3%)
  between operations  0.83 us (1%)
    all_to_all x2, starting transfers between devices, exchange(): return lax.all_to_all(pieces, TORUS, 0, 0, tiled=True)  26.5 us
    ppermute x6, starting transfers between devices, along_x(): return lax.ppermute(value, 'x', [(at, (at + shift) % 4) for at in range(4)])  21 us
    all_to_all x2, waiting for transfers between devices, exchange(): return lax.all_to_all(pieces, TORUS, 0, 0, tiled=True)  9.87 us
    ppermute x2, starting transfers between devices, swap(): return lax.ppermute(value, 'c', [(0, 1), (1, 0)])  3.84 us
    pallas_call x1, Pallas kernels, body(): call(pair_terms, [sds((16, 4, rows, cols), BF16)] * 4, [VMEM, VMEM, VMEM]...  2.68 us
    pallas_call x1, Pallas kernels, body(): call(prepare, (sds((64 * rows, cols), BF16), sds((tokens, width // 2 + co...  2.25 us
    pallas_call x1, Pallas kernels, body(): call(functools.partial(weight_half, 1), (sds((tokens, cols), BF16), sds((...  2.14 us
    convert_element_type x1, other arithmetic, body(): sums = sums.astype(BF16).reshape(64, rows, cols)  1.92 us
  transfers between devices with their start and end apart: 10, of which 3 were waited for; matrix products, arithmetic and copies ran while one was open for 3% of the time, Pallas kernels for 10%

profile of v3, /device:TPU:2, one launch (start us, length us, event | category | flops | bytes accessed | tf_op | source)
XLA Modules:
  0.0 75.4 jit_solution(16393121531381529195)
XLA Ops:
  0.7 2.2 %shard_map.67 = (bf16[512,256]{1,0:T(8,128)(2,1)}, bf16[256,2304]{1,0:T(8,128)(2,1)}) custom-call(bf16[256,4096]{1,0:T(8,128)(2,1)} %hidden.7, bf16[8,256]{1,0:T(8,128)(2,1)} %codes.1, f32[2,256]{1,0:T(2,128)} %scales.1, bf16[256,256]{1,0:T(8,128)(2,1)} %cotangent.7), custom_call_target="tpu_custom_call" | custom-call | bytes 3145728 | tf_op jit(solution)/shard_map/pallas_call | solution.py:153
  2.9 1.9 %collective-permute-start = (bf16[256,2304]{1,0:T(8,128)(2,1)}, bf16[256,2304]{1,0:T(8,128)(2,1)}, u32[]{:S(2)}, u32[]{:S(2)}) collective-permute-start(bf16[256,2304]{1,0:T(8,128)(2,1)} %get-tuple-element.18), channel_id=1, source_target_pairs={{0,1},{1,0},{2,3},{3,2},{4,5},{5,4},{6,7},{7,6},{8,9},{9,8},{10,11... | collective-permute-start | bytes 3538952 | tf_op jit(solution)/shard_map/ppermute | solution.py:24
  4.8 16.6 %all-to-all-start = ((bf16[64,8,256]{2,1,0:T(8,128)(2,1)}), bf16[64,8,256]{2,1,0:T(8,128)(2,1)S(1)}, u32[]{:S(2)}, u32[]{:S(2)}) async-start(bf16[64,8,256]{2,1,0:T(8,128)(2,1)} %bitcast.7), calls=%async_computation | async-start | bytes 524288 | tf_op jit(solution)/shard_map/all_to_all | solution.py:20
  21.4 0.0 collective-permute-done.got
  21.5 2.7 %shard_map.68 = (bf16[16,4,8,256]{3,2,1,0:T(8,128)(2,1)S(1)}, bf16[16,4,8,256]{3,2,1,0:T(8,128)(2,1)}, bf16[16,4,8,256]{3,2,1,0:T(8,128)(2,1)}, bf16[16,4,8,256]{3,2,1,0:T(8,128)(2,1)}) custom-call(bf16[256,4096]{1,0:T(8,128)(2,1)S(1)} %copy-done, bf16[256,256]{1,0:T(8,128)(2,1)S(1)} %copy-done.1, bf16[256,2304]{1,0:T(8,128)(2,1)} %collective-permute-done.got), custom_call_target="tpu_custom_call" | custom-call | flops 536870912 | bytes 4194304 | tf_op jit(solution)/shard_map/pallas_call | solution.py:173
  24.2 3.4 %collective-permute-start.1 = (bf16[16,4,8,256]{3,2,1,0:T(8,128)(2,1)}, bf16[16,4,8,256]{3,2,1,0:T(8,128)(2,1)S(1)}, u32[]{:S(2)}, u32[]{:S(2)}) collective-permute-start(bf16[16,4,8,256]{3,2,1,0:T(8,128)(2,1)} %get-tuple-element.20), channel_id=1, source_target_pairs={{0,128},{128,256},{256,384},{384,0},{1,129},{129,257},{257,385},{3... | collective-permute-start | bytes 786440 | tf_op jit(solution)/shard_map/ppermute | solution.py:28
  27.6 3.0 %collective-permute-start.2 = (bf16[16,4,8,256]{3,2,1,0:T(8,128)(2,1)}, bf16[16,4,8,256]{3,2,1,0:T(8,128)(2,1)}, u32[]{:S(2)}, u32[]{:S(2)}) collective-permute-start(bf16[16,4,8,256]{3,2,1,0:T(8,128)(2,1)} %get-tuple-element.21), channel_id=1, source_target_pairs={{0,256},{128,384},{256,0},{384,128},{1,257},{129,385},{257,1},{385... | collective-permute-start | bytes 786440 | tf_op jit(solution)/shard_map/ppermute | solution.py:28
  30.6 4.0 %collective-permute-start.3 = (bf16[16,4,8,256]{3,2,1,0:T(8,128)(2,1)}, bf16[16,4,8,256]{3,2,1,0:T(8,128)(2,1)}, u32[]{:S(2)}, u32[]{:S(2)}) collective-permute-start(bf16[16,4,8,256]{3,2,1,0:T(8,128)(2,1)} %get-tuple-element.22), channel_id=1, source_target_pairs={{0,384},{128,0},{256,128},{384,256},{1,385},{129,1},{257,129},{385... | collective-permute-start | bytes 786440 | tf_op jit(solution)/shard_map/ppermute | solution.py:28
  34.7 2.6 %all-to-all-done = bf16[64,8,256]{2,1,0:T(8,128)(2,1)S(1)} async-done(((bf16[64,8,256]{2,1,0:T(8,128)(2,1)}), bf16[64,8,256]{2,1,0:T(8,128)(2,1)S(1)}, u32[]{:S(2)}, u32[]{:S(2)}) %all-to-all-start) | async-done | bytes 262176 | tf_op jit(solution)/shard_map/all_to_all | solution.py:20
  37.2 2.4 %collective-permute-start.6 = (bf16[16,4,8,256]{3,2,1,0:T(8,128)(2,1)S(1)}, bf16[16,4,8,256]{3,2,1,0:T(8,128)(2,1)S(1)}, u32[]{:S(2)}, u32[]{:S(2)}) collective-permute-start(bf16[16,4,8,256]{3,2,1,0:T(8,128)(2,1)S(1)} %bitcast.3), channel_id=1, source_target_pairs={{0,384},{128,0},{256,128},{384,256},{1,385},{129,1},{257,129},{385... | collective-permute-start | bytes 786440 | tf_op jit(solution)/shard_map/ppermute | solution.py:28
  39.7 4.3 %collective-permute-start.5 = (bf16[16,4,8,256]{3,2,1,0:T(8,128)(2,1)S(1)}, bf16[16,4,8,256]{3,2,1,0:T(8,128)(2,1)S(1)}, u32[]{:S(2)}, u32[]{:S(2)}) collective-permute-start(bf16[16,4,8,256]{3,2,1,0:T(8,128)(2,1)S(1)} %bitcast.4), channel_id=1, source_target_pairs={{0,256},{128,384},{256,0},{384,128},{1,257},{129,385},{257,1},{385... | collective-permute-start | bytes 786440 | tf_op jit(solution)/shard_map/ppermute | solution.py:28
  44.0 0.0 collective-permute-done.1
  44.0 3.7 %collective-permute-start.4 = (bf16[16,4,8,256]{3,2,1,0:T(8,128)(2,1)S(1)}, bf16[16,4,8,256]{3,2,1,0:T(8,128)(2,1)}, u32[]{:S(2)}, u32[]{:S(2)}) collective-permute-start(bf16[16,4,8,256]{3,2,1,0:T(8,128)(2,1)S(1)} %bitcast.5), channel_id=1, source_target_pairs={{0,128},{128,256},{256,384},{384,0},{1,129},{129,257},{257,385},{3... | collective-permute-start | bytes 786440 | tf_op jit(solution)/shard_map/ppermute | solution.py:28
  47.7 0.0 collective-permute-done.2
  47.8 1.9 %add_convert_fusion = bf16[16,4,8,256]{3,2,1,0:T(8,128)(2,1)} fusion(bf16[16,4,8,256]{3,2,1,0:T(8,128)(2,1)} %collective-permute-done.3, bf16[16,4,8,256]{3,2,1,0:T(8,128)(2,1)} %collective-permute-done.2, bf16[16,4,8,256]{3,2,1,0:T(8,128)(2,1)S(1)} %collective-permute-done.1, bf16[16,4,8,256]{3,2,1,0:T(8,128)(2,1)S(1)} %get-tuple-element.23), kind=kLoop, calls=%fused_computation.1 | loop fusion | flops 1048576 | bytes 1310720 | tf_op jit(solution)/shard_map/convert_element_type | solution.py:189
  49.7 9.9 %all-to-all-start.1 = ((bf16[64,8,256]{2,1,0:T(8,128)(2,1)}), bf16[64,8,256]{2,1,0:T(8,128)(2,1)S(1)}, u32[]{:S(2)}, u32[]{:S(2)}) async-start(bf16[64,8,256]{2,1,0:T(8,128)(2,1)} %bitcast.1), calls=%async_computation.1 | async-start | bytes 524288 | tf_op jit(solution)/shard_map/all_to_all | solution.py:20
  59.6 0.0 collective-permute-done.5.piece2
  59.6 1.1 %shard_map.69.rows = bf16[4,512,256]{2,1,0:T(8,128)(2,1)S(1)} custom-call(bf16[16,4,8,256]{3,2,1,0:T(8,128)(2,1)S(1)} %bitcast.6, bf16[16,4,8,256]{3,2,1,0:T(8,128)(2,1)} %collective-permute-done.4.piece1, bf16[16,4,8,256]{3,2,1,0:T(8,128)(2,1)S(1)} %collective-permute-done.5.piece2, bf16[16,4,8,256]{3,2,1,0:T(8,128)(2,1)S(1)} %collective-permute-done.6.piece3), custom_call_target="tpu_custom_call" | custom-call | bytes 2097152 | tf_op jit(solution)/shard_map/pallas_call | solution.py:191
  60.7 1.9 %collective-permute-start.7 = (bf16[4,512,256]{2,1,0:T(8,128)(2,1)S(1)}, bf16[4,512,256]{2,1,0:T(8,128)(2,1)S(1)}, u32[]{:S(2)}, u32[]{:S(2)}) collective-permute-start(bf16[4,512,256]{2,1,0:T(8,128)(2,1)S(1)} %shard_map.69.rows), channel_id=1, source_target_pairs={{0,1},{1,0},{2,3},{3,2},{4,5},{5,4},{6,7},{7,6},{8,9},{9,8},{10,11... | collective-permute-start | bytes 3145736 | tf_op jit(solution)/shard_map/ppermute | solution.py:24
  62.7 1.5 %shard_map.70 = (f32[256,256]{1,0:T(8,128)S(1)}, bf16[256,4096]{1,0:T(8,128)(2,1)}) custom-call(bf16[256,4096]{1,0:T(8,128)(2,1)S(1)} %copy-done, bf16[256,256]{1,0:T(8,128)(2,1)S(1)} %copy-done.1, bf16[4,512,256]{2,1,0:T(8,128)(2,1)S(1)} %shard_map.69.rows), custom_call_target="tpu_custom_call" | custom-call | flops 53687091200 | bytes 4194304 | tf_op jit(solution)/shard_map/pallas_call | solution.py:206
  64.1 1.1 %collective-permute-done.7.rows = bf16[4,512,256]{2,1,0:T(8,128)(2,1)S(1)} collective-permute-done((bf16[4,512,256]{2,1,0:T(8,128)(2,1)S(1)}, bf16[4,512,256]{2,1,0:T(8,128)(2,1)S(1)}, u32[]{:S(2)}, u32[]{:S(2)}) %collective-permute-start.7) | collective-permute-done | bytes 1048608 | tf_op jit(solution)/shard_map/ppermute | solution.py:24
  65.3 2.1 %shard_map.71 = (bf16[256,256]{1,0:T(8,128)(2,1)}, bf16[256,4096]{1,0:T(8,128)(2,1)}) custom-call(bf16[256,4096]{1,0:T(8,128)(2,1)S(1)} %copy-done, bf16[256,256]{1,0:T(8,128)(2,1)S(1)} %copy-done.1, bf16[4,512,256]{2,1,0:T(8,128)(2,1)S(1)} %collective-permute-done.7.rows, ...), custom_call_target="tpu_custom_call", output_to_operand_aliasing={{1}: (4, {})} | custom-call | flops 536870912 | bytes 4194304 | tf_op jit(solution)/shard_map/pallas_call | solution.py:215
  67.4 7.3 %all-to-all-done.1 = bf16[64,8,256]{2,1,0:T(8,128)(2,1)S(1)} async-done(((bf16[64,8,256]{2,1,0:T(8,128)(2,1)}), bf16[64,8,256]{2,1,0:T(8,128)(2,1)S(1)}, u32[]{:S(2)}, u32[]{:S(2)}) %all-to-all-start.1) | async-done | bytes 262176 | tf_op jit(solution)/shard_map/all_to_all | solution.py:20
  74.7 0.7 convert_reduce_fusion
  (7 shorter events, 0.0 us)
Async XLA Ops:
  0.6 20.8 %copy-start.1 = (bf16[256,256]{1,0:T(8,128)(2,1)S(1)}, bf16[256,256]{1,0:T(8,128)(2,1)}, u32[]{:S(2)}) copy-start(bf16[256,256]{1,0:T(8,128)(2,1)} %cotangent.7) | copy-start | bytes 393220
  0.6 20.8 %copy-start = (bf16[256,4096]{1,0:T(8,128)(2,1)S(1)}, bf16[256,4096]{1,0:T(8,128)(2,1)}, u32[]{:S(2)}) copy-start(bf16[256,4096]{1,0:T(8,128)(2,1)} %hidden.7) | copy-start | bytes 6291460
  2.9 18.5 %collective-permute-start = (bf16[256,2304]{1,0:T(8,128)(2,1)}, bf16[256,2304]{1,0:T(8,128)(2,1)}, u32[]{:S(2)}, u32[]{:S(2)}) collective-permute-start(bf16[256,2304]{1,0:T(8,128)(2,1)} %get-tuple-element.18), channel_id=1, source_target_pairs={{0,1},{1,0},{2,3},{3,2},{4,5},{5,4},{6,7},{7,6},{8,9},{9,8},{10,11... | collective-permute-start | bytes 3538952 | tf_op jit(solution)/shard_map/ppermute | solution.py:24
  4.8 32.4 %all-to-all-start = ((bf16[64,8,256]{2,1,0:T(8,128)(2,1)}), bf16[64,8,256]{2,1,0:T(8,128)(2,1)S(1)}, u32[]{:S(2)}, u32[]{:S(2)}) async-start(bf16[64,8,256]{2,1,0:T(8,128)(2,1)} %bitcast.7), calls=%async_computation | async-start | bytes 524288 | tf_op jit(solution)/shard_map/all_to_all | solution.py:20
  24.2 19.9 %collective-permute-start.1 = (bf16[16,4,8,256]{3,2,1,0:T(8,128)(2,1)}, bf16[16,4,8,256]{3,2,1,0:T(8,128)(2,1)S(1)}, u32[]{:S(2)}, u32[]{:S(2)}) collective-permute-start(bf16[16,4,8,256]{3,2,1,0:T(8,128)(2,1)} %get-tuple-element.20), channel_id=1, source_target_pairs={{0,128},{128,256},{256,384},{384,0},{1,129},{129,257},{257,385},{3... | collective-permute-start | bytes 786440 | tf_op jit(solution)/shard_map/ppermute | solution.py:28
  27.6 20.2 %collective-permute-start.2 = (bf16[16,4,8,256]{3,2,1,0:T(8,128)(2,1)}, bf16[16,4,8,256]{3,2,1,0:T(8,128)(2,1)}, u32[]{:S(2)}, u32[]{:S(2)}) collective-permute-start(bf16[16,4,8,256]{3,2,1,0:T(8,128)(2,1)} %get-tuple-element.21), channel_id=1, source_target_pairs={{0,256},{128,384},{256,0},{384,128},{1,257},{129,385},{257,1},{385... | collective-permute-start | bytes 786440 | tf_op jit(solution)/shard_map/ppermute | solution.py:28
  30.6 17.1 %collective-permute-start.3 = (bf16[16,4,8,256]{3,2,1,0:T(8,128)(2,1)}, bf16[16,4,8,256]{3,2,1,0:T(8,128)(2,1)}, u32[]{:S(2)}, u32[]{:S(2)}) collective-permute-start(bf16[16,4,8,256]{3,2,1,0:T(8,128)(2,1)} %get-tuple-element.22), channel_id=1, source_target_pairs={{0,384},{128,0},{256,128},{384,256},{1,385},{129,1},{257,129},{385... | collective-permute-start | bytes 786440 | tf_op jit(solution)/shard_map/ppermute | solution.py:28
  37.2 22.4 %collective-permute-start.6 = (bf16[16,4,8,256]{3,2,1,0:T(8,128)(2,1)S(1)}, bf16[16,4,8,256]{3,2,1,0:T(8,128)(2,1)S(1)}, u32[]{:S(2)}, u32[]{:S(2)}) collective-permute-start(bf16[16,4,8,256]{3,2,1,0:T(8,128)(2,1)S(1)} %bitcast.3), channel_id=1, source_target_pairs={{0,384},{128,0},{256,128},{384,256},{1,385},{129,1},{257,129},{385... | collective-permute-start | bytes 786440 | tf_op jit(solution)/shard_map/ppermute | solution.py:28
  39.7 19.9 %collective-permute-start.5 = (bf16[16,4,8,256]{3,2,1,0:T(8,128)(2,1)S(1)}, bf16[16,4,8,256]{3,2,1,0:T(8,128)(2,1)S(1)}, u32[]{:S(2)}, u32[]{:S(2)}) collective-permute-start(bf16[16,4,8,256]{3,2,1,0:T(8,128)(2,1)S(1)} %bitcast.4), channel_id=1, source_target_pairs={{0,256},{128,384},{256,0},{384,128},{1,257},{129,385},{257,1},{385... | collective-permute-start | bytes 786440 | tf_op jit(solution)/shard_map/ppermute | solution.py:28
  44.0 15.6 %collective-permute-start.4 = (bf16[16,4,8,256]{3,2,1,0:T(8,128)(2,1)S(1)}, bf16[16,4,8,256]{3,2,1,0:T(8,128)(2,1)}, u32[]{:S(2)}, u32[]{:S(2)}) collective-permute-start(bf16[16,4,8,256]{3,2,1,0:T(8,128)(2,1)S(1)} %bitcast.5), channel_id=1, source_target_pairs={{0,128},{128,256},{256,384},{384,0},{1,129},{129,257},{257,385},{3... | collective-permute-start | bytes 786440 | tf_op jit(solution)/shard_map/ppermute | solution.py:28
  49.7 25.0 %all-to-all-start.1 = ((bf16[64,8,256]{2,1,0:T(8,128)(2,1)}), bf16[64,8,256]{2,1,0:T(8,128)(2,1)S(1)}, u32[]{:S(2)}, u32[]{:S(2)}) async-start(bf16[64,8,256]{2,1,0:T(8,128)(2,1)} %bitcast.1), calls=%async_computation.1 | async-start | bytes 524288 | tf_op jit(solution)/shard_map/all_to_all | solution.py:20
  60.7 4.6 %collective-permute-start.7 = (bf16[4,512,256]{2,1,0:T(8,128)(2,1)S(1)}, bf16[4,512,256]{2,1,0:T(8,128)(2,1)S(1)}, u32[]{:S(2)}, u32[]{:S(2)}) collective-permute-start(bf16[4,512,256]{2,1,0:T(8,128)(2,1)S(1)} %shard_map.69.rows), channel_id=1, source_target_pairs={{0,1},{1,0},{2,3},{3,2},{4,5},{5,4},{6,7},{7,6},{8,9},{9,8},{10,11... | collective-permute-start | bytes 3145736 | tf_op jit(solution)/shard_map/ppermute | solution.py:24
